TPU v7x, 32 devices: a whole 2x2x4 slice. The times are simulated.
32 devices in a mesh: row: 8 (over z, core), col: 4 (over y, x).
Axes of the slice: x: 2, y: 2, z: 4, core: 2. Of those that a mesh axis runs over, the one named last changes fastest.
Arguments:
- panel_diag: float32 [512, 512], P('row'), may hold values from -12 to 150, as said below
- panel_below: float32 [4096, 512], P(('row', 'col')), may hold values from -6 to 6
- trailing: float32 [4096, 4096], P('row', 'col'), may hold values from -6 to 6
- recon_top: float32 [512, 12288], P(None, 'col'), may hold values from -6 to 6
- recon_rest: float32 [4096, 12288], P('row', 'col'), may hold values from -6 to 6
Outputs:
- diag_factor: float32 [512, 512], replicated
- below_factor: float32 [4096, 512], P(('row', 'col'))
- trailing_new: float32 [4096, 4096], P('row', 'col')
- top_solved: float32 [512, 12288], P(None, 'col')
- rest_new: float32 [4096, 12288], P('row', 'col')
Inputs may be any that keep to these rules, and one draw needn't show every extreme that they name: panel_diag is symmetric with a positive diagonal that dominates its spectrum, so it is positive definite.
All inputs are finite; a program needn't handle non-finite values.
Results may differ from a plain program's by a relative error of at most 0.00007.
Values sent between devices are 32-bit elements; how exact they have to be, the bound alone decides.
A program may use at most 128 MiB of HBM per device.

v0:
```python
import functools

import jax
import jax.numpy as jnp
from jax import lax
from jax.experimental import pallas as pl
from jax.experimental.pallas import tpu as pltpu
from jax.sharding import PartitionSpec as P

HI = lax.Precision.HIGHEST
MESH = pl.DeviceIdType.MESH
BLOCK = 128
SUB = 8


def mm(a, b, dims, precision=HI):
    return lax.dot_general(a, b, (dims, ((), ())), precision=precision, preferred_element_type=jnp.float32)

def factor_block(mat, tick):
    row_id = lax.broadcasted_iota(jnp.int32, (SUB, BLOCK), 0)
    lane_id = lax.broadcasted_iota(jnp.int32, (SUB, BLOCK), 1)
    steps = BLOCK // SUB
    d = mat
    uppers, invs = [], []
    g = None
    for s in range(steps):
        base = s * SUB
        rows = d[:SUB, :]
        eye = jnp.where(lane_id == row_id + base, 1.0, 0.0).astype(jnp.float32)
        if g is None:
            grows = eye
        else:
            grows = g[:SUB, :] + eye
        r = [jnp.broadcast_to(rows[j:j+1, :], (SUB, BLOCK)) for j in range(SUB)]
        q = [jnp.broadcast_to(grows[j:j+1, :], (SUB, BLOCK)) for j in range(SUB)]
        S = {}
        for j in range(SUB):
            for k in range(j, SUB):
                S[j, k] = jnp.broadcast_to(r[j][:, base+k:base+k+1], (SUB, BLOCK))
        for j in range(SUB):
            inv = lax.rsqrt(S[j, j])
            c = [None] * SUB
            for k in range(j + 1, SUB):
                c[k] = S[j, k] * inv
            r[j] = r[j] * inv
            q[j] = q[j] * inv
            for i in range(j + 1, SUB):
                for k in range(i, SUB):
                    S[i, k] = S[i, k] - c[i] * c[k]
                r[i] = r[i] - c[i] * r[j]
                q[i] = q[i] - c[i] * q[j]
        u = r[0]
        v = q[0]
        for j in range(1, SUB):
            u = jnp.where(row_id == j, r[j], u)
            v = jnp.where(row_id == j, q[j], v)
        u = jnp.where(lane_id >= row_id + base, u, 0.0)
        uppers.append(u)
        invs.append(v)
        tick()
        if s + 1 < steps:
            both = jnp.concatenate([u, v], axis=1)
            upd = mm(u, both, ((0,), (0,)))
            d = d[SUB:, :] - upd[base+SUB:, :BLOCK]
            g = -upd[base+SUB:, BLOCK:] if g is None else g[SUB:, :] - upd[base+SUB:, BLOCK:]
    return jnp.concatenate(uppers, 0), jnp.concatenate(invs, 0)


def factor_kernel(rows_n, cols_n, a_ref, pb_ref, l_ref, inv_ref, pr_ref, pc_ref, w, y,
                  d_send, d_recv, x_send, x_recv, s_send, s_recv, c_send, c_recv, b_send, b_recv):
    n = w.shape[0]
    chips = rows_n // 2
    piece = n // rows_n
    tall = pb_ref.shape[0]
    block_rows = pr_ref.shape[0]
    ratio = pc_ref.shape[0] // block_rows
    r = lax.axis_index("row")
    c = lax.axis_index("col")
    z = r // 2
    k = lax.rem(r, 2)
    sibling = z * 2 + (1 - k)

    barrier = pltpu.get_barrier_semaphore()
    for step in range(1, rows_n):
        pl.semaphore_signal(barrier, inc=1, device_id=(lax.rem(r + step, rows_n), c), device_id_type=MESH)
    for step in range(1, cols_n):
        pl.semaphore_signal(barrier, inc=1, device_id=(r, lax.rem(c + step, cols_n)), device_id_type=MESH)
    w[pl.ds(pl.multiple_of(r * piece, piece), piece), :] = a_ref[...]
    pr_ref[pl.ds(pl.multiple_of(c * tall, tall), tall), :] = pb_ref[...]
    pl.semaphore_wait(barrier, rows_n + cols_n - 2)

    messages = []
    for p in range(chips):
        lo = p * 2 * piece // BLOCK * BLOCK
        if p == 0:
            messages.append((0, 0, BLOCK))
            lo = BLOCK
        if lo < n:
            messages.append((p, lo, n))

    def diag_copy(m, row, to_row, send, recv):
        p, lo, hi = messages[m]
        part = w.at[pl.ds(pl.multiple_of(row * piece, piece), piece), lo:hi]
        return pltpu.make_async_remote_copy(src_ref=part, dst_ref=part, send_sem=send, recv_sem=recv,
                                            device_id=(to_row, c), device_id_type=MESH)

    def along(m, step):
        to = lax.rem(z + step, chips) * 2 + k
        return diag_copy(m, r, to, d_send.at[m, step - 1], d_recv.at[m])

    def across(m):
        return diag_copy(m, messages[m][0] * 2 + k, sibling, x_send.at[m], x_recv.at[m])

    for m in range(len(messages)):
        @pl.when(z == messages[m][0])
        def _():
            for step in range(1, chips):
                along(m, step).start()

    passed = set()

    def pass_across(m):
        if m in passed:
            return
        passed.add(m)

        @pl.when(z != messages[m][0])
        def _():
            diag_copy(m, messages[m][0] * 2 + k, sibling, d_send.at[m, 0], d_recv.at[m]).wait_recv()
        across(m).start()

    def have(m):
        pass_across(m)
        part = diag_copy(m, messages[m][0] * 2 + (1 - k), sibling, x_send.at[m], x_recv.at[m])
        part.wait_recv()

    def in_row(step):
        part = pr_ref.at[pl.ds(pl.multiple_of(c * tall, tall), tall)]
        return pltpu.make_async_remote_copy(
            src_ref=part, dst_ref=part, send_sem=s_send.at[step - 1], recv_sem=s_recv.at[step - 1],
            device_id=(r, lax.rem(c - step + cols_n, cols_n)), device_id_type=MESH)

    def in_row_wait(step):
        part = pr_ref.at[pl.ds(pl.multiple_of(lax.rem(c + step, cols_n) * tall, tall), tall)]
        pltpu.make_async_remote_copy(
            src_ref=part, dst_ref=part, send_sem=s_send.at[step - 1], recv_sem=s_recv.at[step - 1],
            device_id=(r, lax.rem(c + step, cols_n)), device_id_type=MESH).wait_recv()

    home = c * ratio // 2

    def piece_at(j, core):
        first = lax.rem(c + j, cols_n) * tall
        base = core * block_rows if ratio == 2 else 0
        return pl.multiple_of(base + first, tall)

    def line_copy(j, to, send, recv, core):
        part = pc_ref.at[pl.ds(piece_at(j, core), tall)]
        return pltpu.make_async_remote_copy(src_ref=part, dst_ref=part, send_sem=send, recv_sem=recv,
                                            device_id=(to, c), device_id_type=MESH)

    def down(j):
        return line_copy(j, r + 2, c_send.at[j], c_recv.at[j], k)

    def swap(j, core):
        return line_copy(j, sibling, b_send.at[j], b_recv.at[j], core)

    holds = (z >= home) if ratio == 2 else (z >= home) & (lax.rem(c, 2) == k)
    takes = (z >= home) if ratio == 2 else (z >= home) & (lax.rem(c, 2) != k)

    def line_step(j, hop):
        @pl.when((z - home == hop) & holds)
        def _():
            if hop == 0:
                first = pl.multiple_of(lax.rem(c + j, cols_n) * tall, tall)
                pc_ref[pl.ds(piece_at(j, k), tall), :] = pr_ref[pl.ds(first, tall), :]
            else:
                down(j).wait_recv()
            @pl.when(z < chips - 1)
            def _():
                down(j).start()
            swap(j, k).start()

    ticks = n // SUB
    actions = {}
    span = cols_n + chips - 1
    for m in range(1, len(messages)):
        actions.setdefault(4 * m - 1, []).append(functools.partial(pass_across, m))
    for t in range(span):
        at = 2 + t * (ticks - 8) // (span - 1)
        if 0 < t < cols_n:
            actions.setdefault(at, []).append(functools.partial(in_row_wait, t))
        for j in range(cols_n):
            hop = t - j
            if 0 <= hop < chips:
                actions.setdefault(at, []).append(functools.partial(line_step, j, hop))
    count = [0]

    def tick():
        for action in actions.get(count[0], ()):
            action()
        count[0] += 1

    pass_across(0)
    for step in range(1, cols_n):
        in_row(step).start()
    y[...] = jnp.zeros_like(y)
    l_ref[...] = jnp.zeros_like(l_ref)
    have(0)
    waited = {0}
    for p in range(n // BLOCK):
        lo, hi = p * BLOCK, (p + 1) * BLOCK
        for m in range(len(messages)):
            if m not in waited and messages[m][0] * 2 * piece < hi and (p or messages[m][1] == 0):
                have(m)
                waited.add(m)
        now = w[lo:hi, lo:] if p else w[lo:hi, lo:hi]
        if p:
            before = l_ref[lo:, :lo]
            now = now - mm(l_ref[lo:hi, :lo], before, ((1,), (1,)))
        u, v = factor_block(now[:, :BLOCK], tick)
        l_ref[lo:hi, lo:hi] = u.T
        if p:
            left = mm(l_ref[lo:hi, :lo], y[:lo, :lo], ((1,), (0,)))
            y[lo:hi, :lo] = -mm(v, left, ((1,), (0,)))
        y[lo:hi, lo:hi] = v
        if hi < n:
            if p == 0:
                for m in range(len(messages)):
                    if m not in waited and messages[m][0] * 2 * piece < hi:
                        have(m)
                        waited.add(m)
                rest = w[lo:hi, hi:]
            else:
                rest = now[:, BLOCK:]
            l_ref[hi:, lo:hi] = mm(v, rest, ((1,), (0,))).T
    inv_ref[...] = y[...]

    for m in range(len(messages)):
        @pl.when(z == messages[m][0])
        def _():
            for step in range(1, chips):
                along(m, step).wait_send()
        across(m).wait_send()
    for step in range(1, cols_n):
        in_row(step).wait_send()
    for j in range(cols_n):
        @pl.when(holds)
        def _():
            @pl.when(z < chips - 1)
            def _():
                down(j).wait_send()
            swap(j, k).wait_send()

        @pl.when(takes)
        def _():
            swap(j, 1 - k).wait_recv()


def split(x):
    high = x.astype(jnp.bfloat16)
    return high, (x - high.astype(jnp.float32)).astype(jnp.bfloat16)


def dot3(a, b, dims):
    def one(p, q):
        return lax.dot_general(p, q, (dims, ((), ())), preferred_element_type=jnp.float32)
    return one(a[0], b[0]) + (one(a[0], b[1]) + one(a[1], b[0]))


ROWS = ((1,), (0,))
COLS = ((1,), (1,))


def update_kernel(wide, deep, pr_ref, pc_ref, inv_ref, pb_ref, top_ref, rest_ref, tr_ref,
                  below_ref, top_out, rest_out, tr_out, xr_hi, xr_lo, xc_hi, xc_lo, iv_hi, iv_lo):
    t = pl.program_id(0)
    r = lax.axis_index("row")
    c = lax.axis_index("col")

    @pl.when(t == 0)
    def _():
        inv = split(inv_ref[...])
        iv_hi[...], iv_lo[...] = inv
        xr_hi[...], xr_lo[...] = split(dot3(split(pr_ref[...]), inv, COLS))
        xc_hi[...], xc_lo[...] = split(dot3(split(pc_ref[...]), inv, COLS))
        below_ref[...] = dot3(split(pb_ref[...]), inv, COLS)

    @pl.when(t < wide)
    def _():
        n = inv_ref.shape[0]
        half = n // 2
        top = split(top_ref[...])
        upper = dot3((iv_hi[:half, :half], iv_lo[:half, :half]), (top[0][:half], top[1][:half]), ROWS)
        lower = dot3((iv_hi[half:, :], iv_lo[half:, :]), top, ROWS)
        top_out[:half, :] = upper
        top_out[half:, :] = lower
        solved = split(jnp.concatenate([upper, lower], 0))
        rest_out[...] = rest_ref[...] - dot3((xr_hi[...], xr_lo[...]), solved, ROWS)

    @pl.when(t >= wide)
    def _():
        height, width = tr_ref.shape
        at = pl.ds(pl.multiple_of((t - wide) * width, width), width)
        product = dot3((xr_hi[...], xr_lo[...]), (xc_hi[at, :], xc_lo[at, :]), COLS)
        row = r * height + lax.broadcasted_iota(jnp.int32, (height, width), 0)
        col = (c * deep + (t - wide)) * width + lax.broadcasted_iota(jnp.int32, (height, width), 1)
        tr_out[...] = jnp.where(col <= row, tr_ref[...] - product, tr_ref[...])


def tile_of(size):
    for width in (512, 384, 256, 128):
        if size % width == 0:
            return width
    return size


def shards(rows_n, cols_n, panel_diag, panel_below, trailing, recon_top, recon_rest):
    n = panel_diag.shape[1]
    height, across = trailing.shape
    slopes = recon_top.shape[1]
    f32 = jnp.float32
    whole = pl.BlockSpec(memory_space=pltpu.VMEM)
    chips = rows_n // 2
    dma = pltpu.SemaphoreType.DMA
    diag_factor, inverse, row_panel, col_panel = pl.pallas_call(
        functools.partial(factor_kernel, rows_n, cols_n),
        out_shape=[jax.ShapeDtypeStruct((n, n), f32), jax.ShapeDtypeStruct((n, n), f32),
                   jax.ShapeDtypeStruct((height, n), f32), jax.ShapeDtypeStruct((across, n), f32)],
        in_specs=[whole] * 2,
        out_specs=[whole] * 4,
        scratch_shapes=[pltpu.VMEM((n, n), f32), pltpu.VMEM((n, n), f32),
                        dma((chips + 1, chips - 1)), dma((chips + 1,)), dma((chips + 1,)), dma((chips + 1,)),
                        dma((cols_n - 1,)), dma((cols_n - 1,)), dma((cols_n,)), dma((cols_n,)),
                        dma((cols_n,)), dma((cols_n,))],
        compiler_params=pltpu.CompilerParams(collective_id=0, has_side_effects=True, vmem_limit_bytes=48 * 2**20),
        name="factor",
    )(panel_diag, panel_below)

    tile, strip = tile_of(slopes), tile_of(across)
    wide, deep = slopes // tile, across // strip
    bf16 = jnp.bfloat16
    recon_at = lambda t: (0, jnp.minimum(t, wide - 1))
    trail_at = lambda t: (0, jnp.maximum(t - wide, 0))
    below, top_solved, rest_new, trailing_new = pl.pallas_call(
        functools.partial(update_kernel, wide, deep),
        grid=(wide + deep,),
        out_shape=[jax.ShapeDtypeStruct(panel_below.shape, f32), jax.ShapeDtypeStruct(recon_top.shape, f32),
                   jax.ShapeDtypeStruct(recon_rest.shape, f32), jax.ShapeDtypeStruct(trailing.shape, f32)],
        in_specs=[whole, whole, whole, whole, pl.BlockSpec((n, tile), recon_at),
                  pl.BlockSpec((height, tile), recon_at), pl.BlockSpec((height, strip), trail_at)],
        out_specs=[whole, pl.BlockSpec((n, tile), recon_at),
                   pl.BlockSpec((height, tile), recon_at), pl.BlockSpec((height, strip), trail_at)],
        scratch_shapes=[pltpu.VMEM((height, n), bf16), pltpu.VMEM((height, n), bf16),
                        pltpu.VMEM((across, n), bf16), pltpu.VMEM((across, n), bf16),
                        pltpu.VMEM((n, n), bf16), pltpu.VMEM((n, n), bf16)],
        compiler_params=pltpu.CompilerParams(vmem_limit_bytes=50 * 2**20),
        name="update",
    )(row_panel, col_panel, inverse, panel_below, recon_top, recon_rest, trailing)
    return (diag_factor, below, trailing_new, top_solved, rest_new)


def solution(mesh):
    rows_n, cols_n = mesh.shape["row"], mesh.shape["col"]
    placed = (
        P("row", None),
        P(("row", "col"), None),
        P("row", "col"),
        P(None, "col"),
        P("row", "col"),
    )
    return jax.shard_map(
        functools.partial(shards, rows_n, cols_n),
        mesh=mesh,
        in_specs=placed,
        out_specs=(P(), P(("row", "col"), None), P("row", "col"), P(None, "col"), P("row", "col")),
        check_vma=False,
    )
```

profile of v0, /device:TPU:24, one launch (start us, length us, event | category | flops | bytes accessed | tf_op | source)
XLA Modules:
  0.0 86.1 jit_solution(18089505563103920973)
XLA Ops:
  0.6 0.0 copy-start.1
  0.6 0.9 %copy-done.1 = f32[128,512]{1,0:T(8,128)S(1)} copy-done((f32[128,512]{1,0:T(8,128)S(1)}, f32[128,512]{1,0:T(8,128)}, u32[]{:S(2)}) %copy-start.1) | copy-done | bytes 262168
  1.6 0.0 copy-start.3
  1.6 0.9 %copy-done.3 = f32[64,512]{1,0:T(8,128)S(1)} copy-done((f32[64,512]{1,0:T(8,128)S(1)}, f32[64,512]{1,0:T(8,128)}, u32[]{:S(2)}) %copy-start.3) | copy-done | bytes 131096
  2.5 58.5 %factor.1 = (f32[512,512]{1,0:T(8,128)S(1)}, f32[512,512]{1,0:T(8,128)S(1)}, f32[512,512]{1,0:T(8,128)S(1)}, f32[1024,512]{1,0:T(8,128)S(1)}) custom-call(f32[64,512]{1,0:T(8,128)S(1)} %copy-done.3, f32[128,512]{1,0:T(8,128)S(1)} %copy-done.1), custom_call_target="tpu_custom_call" | custom-call | tf_op jit(solution)/shard_map/factor/pallas_call | solution.py:325
  61.0 0.0 copy-start
  61.0 1.3 %copy-done = f32[1024,512]{1,0:T(8,128)} copy-done((f32[1024,512]{1,0:T(8,128)}, f32[1024,512]{1,0:T(8,128)S(1)}, u32[]{:S(2)}) %copy-start) | copy-done | bytes 2097176
  62.3 0.0 copy-start.2
  62.3 0.9 %copy-done.2 = f32[128,512]{1,0:T(8,128)S(1)} copy-done((f32[128,512]{1,0:T(8,128)S(1)}, f32[128,512]{1,0:T(8,128)}, u32[]{:S(2)}) %copy-start.2) | copy-done | bytes 262168
  63.3 21.8 %update.1 = (f32[128,512]{1,0:T(8,128)}, f32[512,3072]{1,0:T(8,128)}, f32[512,3072]{1,0:T(8,128)}, f32[512,1024]{1,0:T(8,128)}) custom-call(f32[512,512]{1,0:T(8,128)S(1)} %get-tuple-element.14.pr_ref, f32[1024,512]{1,0:T(8,128)} %copy-done, f32[512,512]{1,0:T(8,128)S(1)} %get-tuple-element.16.inv_ref, f32[128,512]{1,0:T(8,128)S(1)} %copy-done.2, ...), custom_call_target="tpu_custom_call" | custom-call | tf_op jit(solution)/shard_map/update/pallas_call | solution.py:344
  85.1 1.0 %copy.11 = f32[512,512]{1,0:T(8,128)} copy(f32[512,512]{1,0:T(8,128)S(1)} %get-tuple-element.26) | data formatting | bytes 2097152
Async XLA Ops:
  0.6 1.0 %copy-start.1 = (f32[128,512]{1,0:T(8,128)S(1)}, f32[128,512]{1,0:T(8,128)}, u32[]{:S(2)}) copy-start(f32[128,512]{1,0:T(8,128)} %pb_ref.3) | copy-start | bytes 786436
  1.6 0.9 %copy-start.3 = (f32[64,512]{1,0:T(8,128)S(1)}, f32[64,512]{1,0:T(8,128)}, u32[]{:S(2)}) copy-start(f32[64,512]{1,0:T(8,128)} %a_ref.1) | copy-start | bytes 393220
  61.0 1.3 %copy-start = (f32[1024,512]{1,0:T(8,128)}, f32[1024,512]{1,0:T(8,128)S(1)}, u32[]{:S(2)}) copy-start(f32[1024,512]{1,0:T(8,128)S(1)} %get-tuple-element.15.pc_ref) | copy-start | bytes 6291460
  62.3 0.9 %copy-start.2 = (f32[128,512]{1,0:T(8,128)S(1)}, f32[128,512]{1,0:T(8,128)}, u32[]{:S(2)}) copy-start(f32[128,512]{1,0:T(8,128)} %pb_ref.3) | copy-start | bytes 786436
where the time goes:
time: 86.5 us; the launch traced here: 86.1 us
  Pallas kernels  80.3 us (93%)
  local copies, waits for them, and re-layouts  5.1 us (6%)
    pallas_call x1, Pallas kernels, shards(): pl.pallas_call(functools.partial(factor_kernel, rows_n, cols_n), out_shap...  58.5 us
    pallas_call x1, Pallas kernels, shards(): pl.pallas_call(functools.partial(update_kernel, wide, deep), grid=(wide +...  21.8 us
    unnamed x9, local copies, waits for them, and re-layouts  5.1 us

commit v1 on v0

--- a/solution.py
+++ b/solution.py
@@ -13,8 +13,19 @@
 SUB = 8
 
 
-def mm(a, b, dims, precision=HI):
-    return lax.dot_general(a, b, (dims, ((), ())), precision=precision, preferred_element_type=jnp.float32)
+def rounded(x):
+    return x.astype(jnp.bfloat16).astype(jnp.float32)
+
+def mm6(a, b, dims):
+    def parts(x):
+        high = rounded(x)
+        mid = rounded(x - high)
+        return high, mid, (x - high) - mid
+    ah, am, al = parts(a)
+    bh, bm, bl = parts(b)
+    left = jnp.concatenate([ah, ah, am, am, ah, al], axis=dims[0][0]).astype(jnp.bfloat16)
+    right = jnp.concatenate([bh, bm, bh, bm, bl, bh], axis=dims[1][0]).astype(jnp.bfloat16)
+    return lax.dot_general(left, right, (dims, ((), ())), preferred_element_type=jnp.float32)
 
 def factor_block(mat, tick):
     row_id = lax.broadcasted_iota(jnp.int32, (SUB, BLOCK), 0)
@@ -60,14 +71,14 @@
         tick()
         if s + 1 < steps:
             both = jnp.concatenate([u, v], axis=1)
-            upd = mm(u, both, ((0,), (0,)))
+            upd = mm6(u, both, ((0,), (0,)))
             d = d[SUB:, :] - upd[base+SUB:, :BLOCK]
             g = -upd[base+SUB:, BLOCK:] if g is None else g[SUB:, :] - upd[base+SUB:, BLOCK:]
     return jnp.concatenate(uppers, 0), jnp.concatenate(invs, 0)
 
 
 def factor_kernel(rows_n, cols_n, a_ref, pb_ref, l_ref, inv_ref, pr_ref, pc_ref, w, y,
-                  d_send, d_recv, x_send, x_recv, s_send, s_recv, c_send, c_recv, b_send, b_recv):
+                  own, d_send, d_recv, x_send, x_recv, s_send, s_recv, c_send, c_recv, b_send, b_recv):
     n = w.shape[0]
     chips = rows_n // 2
     piece = n // rows_n
@@ -80,13 +91,17 @@
     k = lax.rem(r, 2)
     sibling = z * 2 + (1 - k)
 
+    mine_a = pltpu.make_async_copy(a_ref, w.at[pl.ds(pl.multiple_of(r * piece, piece), piece)], own.at[0])
+    mine_b = pltpu.make_async_copy(pb_ref, pr_ref.at[pl.ds(pl.multiple_of(c * tall, tall), tall)], own.at[1])
+    mine_a.start()
+    mine_b.start()
     barrier = pltpu.get_barrier_semaphore()
     for step in range(1, rows_n):
         pl.semaphore_signal(barrier, inc=1, device_id=(lax.rem(r + step, rows_n), c), device_id_type=MESH)
     for step in range(1, cols_n):
         pl.semaphore_signal(barrier, inc=1, device_id=(r, lax.rem(c + step, cols_n)), device_id_type=MESH)
-    w[pl.ds(pl.multiple_of(r * piece, piece), piece), :] = a_ref[...]
-    pr_ref[pl.ds(pl.multiple_of(c * tall, tall), tall), :] = pb_ref[...]
+    mine_a.wait()
+    mine_b.wait()
     pl.semaphore_wait(barrier, rows_n + cols_n - 2)
 
     messages = []
@@ -216,12 +231,12 @@
         now = w[lo:hi, lo:] if p else w[lo:hi, lo:hi]
         if p:
             before = l_ref[lo:, :lo]
-            now = now - mm(l_ref[lo:hi, :lo], before, ((1,), (1,)))
+            now = now - mm6(l_ref[lo:hi, :lo], before, ((1,), (1,)))
         u, v = factor_block(now[:, :BLOCK], tick)
         l_ref[lo:hi, lo:hi] = u.T
         if p:
-            left = mm(l_ref[lo:hi, :lo], y[:lo, :lo], ((1,), (0,)))
-            y[lo:hi, :lo] = -mm(v, left, ((1,), (0,)))
+            left = mm6(l_ref[lo:hi, :lo], y[:lo, :lo], ((1,), (0,)))
+            y[lo:hi, :lo] = -mm6(v, left, ((1,), (0,)))
         y[lo:hi, lo:hi] = v
         if hi < n:
             if p == 0:
@@ -232,7 +247,7 @@
                 rest = w[lo:hi, hi:]
             else:
                 rest = now[:, BLOCK:]
-            l_ref[hi:, lo:hi] = mm(v, rest, ((1,), (0,))).T
+            l_ref[hi:, lo:hi] = mm6(v, rest, ((1,), (0,))).T
     inv_ref[...] = y[...]
 
     for m in range(len(messages)):
@@ -261,50 +276,66 @@
     return high, (x - high.astype(jnp.float32)).astype(jnp.bfloat16)
 
 
-def dot3(a, b, dims):
-    def one(p, q):
-        return lax.dot_general(p, q, (dims, ((), ())), preferred_element_type=jnp.float32)
-    return one(a[0], b[0]) + (one(a[0], b[1]) + one(a[1], b[0]))
+def left_parts(x, axis):
+    high, low = split(x)
+    return jnp.concatenate([high, high, low], axis=axis)
+
+
+def right_parts(x, axis):
+    high, low = split(x)
+    return jnp.concatenate([high, low, high], axis=axis)
+
+
+def dot(a, b, dims):
+    return lax.dot_general(a, b, (dims, ((), ())), preferred_element_type=jnp.float32)
 
 
 ROWS = ((1,), (0,))
 COLS = ((1,), (1,))
 
 
-def update_kernel(wide, deep, pr_ref, pc_ref, inv_ref, pb_ref, top_ref, rest_ref, tr_ref,
-                  below_ref, top_out, rest_out, tr_out, xr_hi, xr_lo, xc_hi, xc_lo, iv_hi, iv_lo):
+def update_kernel(wide, deep, l_ref, pr_ref, pc_ref, inv_ref, top_ref, rest_ref, tr_ref,
+                  l_out, below_ref, top_out, rest_out, tr_out, xr, xc, iv, iv_top, sem):
     t = pl.program_id(0)
     r = lax.axis_index("row")
     c = lax.axis_index("col")
+    n = inv_ref.shape[0]
+    half = n // 2
+    tall = below_ref.shape[0]
 
     @pl.when(t == 0)
     def _():
-        inv = split(inv_ref[...])
-        iv_hi[...], iv_lo[...] = inv
-        xr_hi[...], xr_lo[...] = split(dot3(split(pr_ref[...]), inv, COLS))
-        xc_hi[...], xc_lo[...] = split(dot3(split(pc_ref[...]), inv, COLS))
-        below_ref[...] = dot3(split(pb_ref[...]), inv, COLS)
+        pltpu.make_async_copy(l_ref, l_out, sem).start()
+        inv = right_parts(inv_ref[...], 1)
+        xr[...] = left_parts(dot(left_parts(pr_ref[...], 1), inv, COLS), 1)
+        xc[...] = right_parts(dot(left_parts(pc_ref[...], 1), inv, COLS), 1)
+        own = pr_ref[pl.ds(pl.multiple_of(c * tall, tall), tall), :]
+        below_ref[...] = dot(left_parts(own, 1), inv, COLS)
+        iv[...] = left_parts(inv_ref[half:, :], 1)
+        iv_top[...] = left_parts(inv_ref[:half, :half], 1)
 
     @pl.when(t < wide)
     def _():
-        n = inv_ref.shape[0]
-        half = n // 2
-        top = split(top_ref[...])
-        upper = dot3((iv_hi[:half, :half], iv_lo[:half, :half]), (top[0][:half], top[1][:half]), ROWS)
-        lower = dot3((iv_hi[half:, :], iv_lo[half:, :]), top, ROWS)
+        top = top_ref[...]
+        upper = dot(iv_top[...], right_parts(top[:half], 0), ROWS)
+        lower = dot(iv[...], right_parts(top, 0), ROWS)
         top_out[:half, :] = upper
         top_out[half:, :] = lower
-        solved = split(jnp.concatenate([upper, lower], 0))
-        rest_out[...] = rest_ref[...] - dot3((xr_hi[...], xr_lo[...]), solved, ROWS)
+        solved = right_parts(jnp.concatenate([upper, lower], 0), 0)
+        rest_out[...] = rest_ref[...] - dot(xr[...], solved, ROWS)
 
     @pl.when(t >= wide)
     def _():
         height, width = tr_ref.shape
         at = pl.ds(pl.multiple_of((t - wide) * width, width), width)
-        product = dot3((xr_hi[...], xr_lo[...]), (xc_hi[at, :], xc_lo[at, :]), COLS)
+        product = dot(xr[...], xc[at, :], COLS)
         row = r * height + lax.broadcasted_iota(jnp.int32, (height, width), 0)
         col = (c * deep + (t - wide)) * width + lax.broadcasted_iota(jnp.int32, (height, width), 1)
         tr_out[...] = jnp.where(col <= row, tr_ref[...] - product, tr_ref[...])
+
+    @pl.when(t == wide + deep - 1)
+    def _():
+        pltpu.make_async_copy(l_ref, l_out, sem).wait()
 
 
 def tile_of(size):
@@ -326,13 +357,13 @@
         functools.partial(factor_kernel, rows_n, cols_n),
         out_shape=[jax.ShapeDtypeStruct((n, n), f32), jax.ShapeDtypeStruct((n, n), f32),
                    jax.ShapeDtypeStruct((height, n), f32), jax.ShapeDtypeStruct((across, n), f32)],
-        in_specs=[whole] * 2,
+        in_specs=[pl.BlockSpec(memory_space=pl.ANY)] * 2,
         out_specs=[whole] * 4,
         scratch_shapes=[pltpu.VMEM((n, n), f32), pltpu.VMEM((n, n), f32),
-                        dma((chips + 1, chips - 1)), dma((chips + 1,)), dma((chips + 1,)), dma((chips + 1,)),
+                        dma((2,)), dma((chips + 1, chips - 1)), dma((chips + 1,)), dma((chips + 1,)), dma((chips + 1,)),
                         dma((cols_n - 1,)), dma((cols_n - 1,)), dma((cols_n,)), dma((cols_n,)),
                         dma((cols_n,)), dma((cols_n,))],
-        compiler_params=pltpu.CompilerParams(collective_id=0, has_side_effects=True, vmem_limit_bytes=48 * 2**20),
+        compiler_params=pltpu.CompilerParams(collective_id=0, has_side_effects=True, vmem_limit_bytes=58 * 2**20),
         name="factor",
     )(panel_diag, panel_below)
 
@@ -341,22 +372,22 @@
     bf16 = jnp.bfloat16
     recon_at = lambda t: (0, jnp.minimum(t, wide - 1))
     trail_at = lambda t: (0, jnp.maximum(t - wide, 0))
-    below, top_solved, rest_new, trailing_new = pl.pallas_call(
+    diag_out, below, top_solved, rest_new, trailing_new = pl.pallas_call(
         functools.partial(update_kernel, wide, deep),
         grid=(wide + deep,),
-        out_shape=[jax.ShapeDtypeStruct(panel_below.shape, f32), jax.ShapeDtypeStruct(recon_top.shape, f32),
+        out_shape=[jax.ShapeDtypeStruct((n, n), f32), jax.ShapeDtypeStruct(panel_below.shape, f32),
+                   jax.ShapeDtypeStruct(recon_top.shape, f32),
                    jax.ShapeDtypeStruct(recon_rest.shape, f32), jax.ShapeDtypeStruct(trailing.shape, f32)],
         in_specs=[whole, whole, whole, whole, pl.BlockSpec((n, tile), recon_at),
                   pl.BlockSpec((height, tile), recon_at), pl.BlockSpec((height, strip), trail_at)],
-        out_specs=[whole, pl.BlockSpec((n, tile), recon_at),
+        out_specs=[pl.BlockSpec(memory_space=pl.ANY), whole, pl.BlockSpec((n, tile), recon_at),
                    pl.BlockSpec((height, tile), recon_at), pl.BlockSpec((height, strip), trail_at)],
-        scratch_shapes=[pltpu.VMEM((height, n), bf16), pltpu.VMEM((height, n), bf16),
-                        pltpu.VMEM((across, n), bf16), pltpu.VMEM((across, n), bf16),
-                        pltpu.VMEM((n, n), bf16), pltpu.VMEM((n, n), bf16)],
-        compiler_params=pltpu.CompilerParams(vmem_limit_bytes=50 * 2**20),
+        scratch_shapes=[pltpu.VMEM((height, 3 * n), bf16), pltpu.VMEM((across, 3 * n), bf16),
+                        pltpu.VMEM((n - n // 2, 3 * n), bf16), pltpu.VMEM((n // 2, 3 * (n // 2)), bf16), dma],
+        compiler_params=pltpu.CompilerParams(vmem_limit_bytes=57 * 2**20),
         name="update",
-    )(row_panel, col_panel, inverse, panel_below, recon_top, recon_rest, trailing)
-    return (diag_factor, below, trailing_new, top_solved, rest_new)
+    )(diag_factor, row_panel, col_panel, inverse, recon_top, recon_rest, trailing)
+    return (diag_out, below, trailing_new, top_solved, rest_new)
 
 
 def solution(mesh):

time: 86.5 us -> 81.3 us (0.940)
  local copies, waits for them, and re-layouts: 5.1 us -> 0 us
    unnamed x9 -> x0, local copies, waits for them, and re-layouts: 5.1 us -> none
where the time goes in v1:
time: 81.3 us; the launch traced here: 81 us
  Pallas kernels  80.2 us (99%)
    pallas_call x1, Pallas kernels, shards(): pl.pallas_call(functools.partial(factor_kernel, rows_n, cols_n), out_shap...  57.7 us
    pallas_call x1, Pallas kernels, shards(): pl.pallas_call(functools.partial(update_kernel, wide, deep), grid=(wide +...  22.5 us

profile of v1, /device:TPU:24, one launch (start us, length us, event | category | flops | bytes accessed | tf_op | source)
XLA Modules:
  0.0 81.0 jit_solution(4167081842167717581)
XLA Ops:
  0.6 57.7 %factor.1 = (f32[512,512]{1,0:T(8,128)}, f32[512,512]{1,0:T(8,128)}, f32[512,512]{1,0:T(8,128)}, f32[1024,512]{1,0:T(8,128)}) custom-call(f32[64,512]{1,0:T(8,128)} %a_ref.1, f32[128,512]{1,0:T(8,128)} %pb_ref.1), custom_call_target="tpu_custom_call" | custom-call | tf_op jit(solution)/shard_map/factor/pallas_call | solution.py:356
  58.3 22.5 %update.1 = (f32[512,512]{1,0:T(8,128)}, f32[128,512]{1,0:T(8,128)}, f32[512,3072]{1,0:T(8,128)}, f32[512,3072]{1,0:T(8,128)}, f32[512,1024]{1,0:T(8,128)}) custom-call(f32[512,512]{1,0:T(8,128)} %get-tuple-element.14.l_ref, f32[512,512]{1,0:T(8,128)} %get-tuple-element.15.pr_ref, f32[1024,512]{1,0:T(8,128)} %get-tuple-element.16.pc_ref, ...), custom_call_target="tpu_custom_call" | custom-call | tf_op jit(solution)/shard_map/update/pallas_call | solution.py:375

commit v2 on v1

--- a/solution.py
+++ b/solution.py
@@ -11,6 +11,7 @@
 MESH = pl.DeviceIdType.MESH
 BLOCK = 128
 SUB = 8
+CUTS = 2
 
 
 def rounded(x):
@@ -83,6 +84,7 @@
     chips = rows_n // 2
     piece = n // rows_n
     tall = pb_ref.shape[0]
+    short = tall // CUTS
     block_rows = pr_ref.shape[0]
     ratio = pc_ref.shape[0] // block_rows
     r = lax.axis_index("row")
@@ -119,33 +121,57 @@
         return pltpu.make_async_remote_copy(src_ref=part, dst_ref=part, send_sem=send, recv_sem=recv,
                                             device_id=(to_row, c), device_id_type=MESH)
 
-    def along(m, step):
-        to = lax.rem(z + step, chips) * 2 + k
-        return diag_copy(m, r, to, d_send.at[m, step - 1], d_recv.at[m])
-
     def across(m):
         return diag_copy(m, messages[m][0] * 2 + k, sibling, x_send.at[m], x_recv.at[m])
 
-    for m in range(len(messages)):
+    def direct(step):
+        to = lax.rem(z + step, chips) * 2 + k
+        return diag_copy(0, r, to, d_send.at[0, step - 1], d_recv.at[0])
+
+    def onward(m, way):
+        row = messages[m][0] * 2 + k
+        return diag_copy(m, row, r + 2 - 4 * way, d_send.at[m, way], d_recv.at[m])
+
+    def goes(m, way):
+        p = messages[m][0]
+        return (z >= p) & (z < chips - 1) if way == 0 else (z <= p) & (z > 0)
+
+    def pass_on(m):
+        for way in range(2):
+            @pl.when(goes(m, way))
+            def _():
+                onward(m, way).start()
+        across(m).start()
+
+    @pl.when(z == 0)
+    def _():
+        for step in range(1, chips):
+            direct(step).start()
+        across(0).start()
+    for m in range(1, len(messages)):
         @pl.when(z == messages[m][0])
         def _():
-            for step in range(1, chips):
-                along(m, step).start()
+            pass_on(m)
 
     passed = set()
 
-    def pass_across(m):
-        if m in passed:
+    def forward(m, hop):
+        if (m, hop) in passed:
             return
-        passed.add(m)
-
-        @pl.when(z != messages[m][0])
+        passed.add((m, hop))
+        p = messages[m][0]
+
+        @pl.when((z == p + hop) | (z == p - hop))
         def _():
-            diag_copy(m, messages[m][0] * 2 + k, sibling, d_send.at[m, 0], d_recv.at[m]).wait_recv()
-        across(m).start()
+            onward(m, 0).wait_recv()
+            if m == 0:
+                across(0).start()
+            else:
+                pass_on(m)
 
     def have(m):
-        pass_across(m)
+        for hop in range(1, chips):
+            forward(m, hop)
         part = diag_copy(m, messages[m][0] * 2 + (1 - k), sibling, x_send.at[m], x_recv.at[m])
         part.wait_recv()
 
@@ -164,12 +190,12 @@
     home = c * ratio // 2
 
     def piece_at(j, core):
-        first = lax.rem(c + j, cols_n) * tall
+        first = lax.rem(c + j // CUTS, cols_n) * tall + j % CUTS * short
         base = core * block_rows if ratio == 2 else 0
-        return pl.multiple_of(base + first, tall)
+        return pl.multiple_of(base + first, short)
 
     def line_copy(j, to, send, recv, core):
-        part = pc_ref.at[pl.ds(piece_at(j, core), tall)]
+        part = pc_ref.at[pl.ds(piece_at(j, core), short)]
         return pltpu.make_async_remote_copy(src_ref=part, dst_ref=part, send_sem=send, recv_sem=recv,
                                             device_id=(to, c), device_id_type=MESH)
 
@@ -186,8 +212,8 @@
         @pl.when((z - home == hop) & holds)
         def _():
             if hop == 0:
-                first = pl.multiple_of(lax.rem(c + j, cols_n) * tall, tall)
-                pc_ref[pl.ds(piece_at(j, k), tall), :] = pr_ref[pl.ds(first, tall), :]
+                first = pl.multiple_of(lax.rem(c + j // CUTS, cols_n) * tall + j % CUTS * short, short)
+                pc_ref[pl.ds(piece_at(j, k), short), :] = pr_ref[pl.ds(first, short), :]
             else:
                 down(j).wait_recv()
             @pl.when(z < chips - 1)
@@ -197,14 +223,15 @@
 
     ticks = n // SUB
     actions = {}
-    span = cols_n + chips - 1
+    span = CUTS * cols_n + chips - 1
     for m in range(1, len(messages)):
-        actions.setdefault(4 * m - 1, []).append(functools.partial(pass_across, m))
+        for hop in range(1, chips):
+            actions.setdefault(3 * m + 3 * hop - 3, []).append(functools.partial(forward, m, hop))
     for t in range(span):
-        at = 2 + t * (ticks - 8) // (span - 1)
-        if 0 < t < cols_n:
-            actions.setdefault(at, []).append(functools.partial(in_row_wait, t))
-        for j in range(cols_n):
+        at = 2 + t * (ticks - 4) // (span - 1)
+        if t % CUTS == 0 and 0 < t // CUTS < cols_n:
+            actions.setdefault(at, []).append(functools.partial(in_row_wait, t // CUTS))
+        for j in range(CUTS * cols_n):
             hop = t - j
             if 0 <= hop < chips:
                 actions.setdefault(at, []).append(functools.partial(line_step, j, hop))
@@ -215,7 +242,8 @@
             action()
         count[0] += 1
 
-    pass_across(0)
+    for hop in range(1, chips):
+        forward(0, hop)
     for step in range(1, cols_n):
         in_row(step).start()
     y[...] = jnp.zeros_like(y)
@@ -250,15 +278,20 @@
             l_ref[hi:, lo:hi] = mm6(v, rest, ((1,), (0,))).T
     inv_ref[...] = y[...]
 
+    @pl.when(z == 0)
+    def _():
+        for step in range(1, chips):
+            direct(step).wait_send()
     for m in range(len(messages)):
-        @pl.when(z == messages[m][0])
-        def _():
-            for step in range(1, chips):
-                along(m, step).wait_send()
+        if m:
+            for way in range(2):
+                @pl.when(goes(m, way))
+                def _():
+                    onward(m, way).wait_send()
         across(m).wait_send()
     for step in range(1, cols_n):
         in_row(step).wait_send()
-    for j in range(cols_n):
+    for j in range(CUTS * cols_n):
         @pl.when(holds)
         def _():
             @pl.when(z < chips - 1)
@@ -295,7 +328,7 @@
 
 
 def update_kernel(wide, deep, l_ref, pr_ref, pc_ref, inv_ref, top_ref, rest_ref, tr_ref,
-                  l_out, below_ref, top_out, rest_out, tr_out, xr, xc, iv, iv_top, sem):
+                  l_out, below_ref, top_out, rest_out, tr_out, weights, iv_top, solved, sem):
     t = pl.program_id(0)
     r = lax.axis_index("row")
     c = lax.axis_index("col")
@@ -306,29 +339,26 @@
     @pl.when(t == 0)
     def _():
         pltpu.make_async_copy(l_ref, l_out, sem).start()
-        inv = right_parts(inv_ref[...], 1)
-        xr[...] = left_parts(dot(left_parts(pr_ref[...], 1), inv, COLS), 1)
-        xc[...] = right_parts(dot(left_parts(pc_ref[...], 1), inv, COLS), 1)
-        own = pr_ref[pl.ds(pl.multiple_of(c * tall, tall), tall), :]
-        below_ref[...] = dot(left_parts(own, 1), inv, COLS)
-        iv[...] = left_parts(inv_ref[half:, :], 1)
-        iv_top[...] = left_parts(inv_ref[:half, :half], 1)
+        inv = inv_ref[...]
+        iv_top[...] = left_parts(inv[:half, :half], 1)
+        weights[:half, :] = left_parts(inv[half:, :], 1)
+        solved[...] = dot(left_parts(pr_ref[...], 1), right_parts(inv, 1), COLS)
+        below_ref[...] = solved[pl.ds(pl.multiple_of(c * tall, tall), tall), :]
+        weights[half:, :] = left_parts(dot(left_parts(solved[...], 1), right_parts(inv, 0), ROWS), 1)
 
     @pl.when(t < wide)
     def _():
-        top = top_ref[...]
-        upper = dot(iv_top[...], right_parts(top[:half], 0), ROWS)
-        lower = dot(iv[...], right_parts(top, 0), ROWS)
-        top_out[:half, :] = upper
-        top_out[half:, :] = lower
-        solved = right_parts(jnp.concatenate([upper, lower], 0), 0)
-        rest_out[...] = rest_ref[...] - dot(xr[...], solved, ROWS)
+        parts = right_parts(top_ref[:half, :], 0)
+        top_out[:half, :] = dot(iv_top[...], parts, ROWS)
+        parts = right_parts(top_ref[...], 0)
+        top_out[half:, :] = dot(weights[:half, :], parts, ROWS)
+        rest_out[...] = rest_ref[...] - dot(weights[half:, :], parts, ROWS)
 
     @pl.when(t >= wide)
     def _():
         height, width = tr_ref.shape
         at = pl.ds(pl.multiple_of((t - wide) * width, width), width)
-        product = dot(xr[...], xc[at, :], COLS)
+        product = dot(weights[half:, :], right_parts(pc_ref[at, :], 1), COLS)
         row = r * height + lax.broadcasted_iota(jnp.int32, (height, width), 0)
         col = (c * deep + (t - wide)) * width + lax.broadcasted_iota(jnp.int32, (height, width), 1)
         tr_out[...] = jnp.where(col <= row, tr_ref[...] - product, tr_ref[...])
@@ -361,8 +391,8 @@
         out_specs=[whole] * 4,
         scratch_shapes=[pltpu.VMEM((n, n), f32), pltpu.VMEM((n, n), f32),
                         dma((2,)), dma((chips + 1, chips - 1)), dma((chips + 1,)), dma((chips + 1,)), dma((chips + 1,)),
-                        dma((cols_n - 1,)), dma((cols_n - 1,)), dma((cols_n,)), dma((cols_n,)),
-                        dma((cols_n,)), dma((cols_n,))],
+                        dma((cols_n - 1,)), dma((cols_n - 1,)), dma((CUTS * cols_n,)), dma((CUTS * cols_n,)),
+                        dma((CUTS * cols_n,)), dma((CUTS * cols_n,))],
         compiler_params=pltpu.CompilerParams(collective_id=0, has_side_effects=True, vmem_limit_bytes=58 * 2**20),
         name="factor",
     )(panel_diag, panel_below)
@@ -382,8 +412,8 @@
                   pl.BlockSpec((height, tile), recon_at), pl.BlockSpec((height, strip), trail_at)],
         out_specs=[pl.BlockSpec(memory_space=pl.ANY), whole, pl.BlockSpec((n, tile), recon_at),
                    pl.BlockSpec((height, tile), recon_at), pl.BlockSpec((height, strip), trail_at)],
-        scratch_shapes=[pltpu.VMEM((height, 3 * n), bf16), pltpu.VMEM((across, 3 * n), bf16),
-                        pltpu.VMEM((n - n // 2, 3 * n), bf16), pltpu.VMEM((n // 2, 3 * (n // 2)), bf16), dma],
+        scratch_shapes=[pltpu.VMEM((n - n // 2 + height, 3 * n), bf16), pltpu.VMEM((n // 2, 3 * (n // 2)), bf16),
+                        pltpu.VMEM((height, n), f32), dma],
         compiler_params=pltpu.CompilerParams(vmem_limit_bytes=57 * 2**20),
         name="update",
     )(diag_factor, row_panel, col_panel, inverse, recon_top, recon_rest, trailing)

time: 81.3 us -> 76.6 us (0.942)
  Pallas kernels: 80.2 us -> 75 us
    pallas_call x1, Pallas kernels: 57.7 us -> 53.7 us  [shards(): pl.pallas_call(functools.partial(factor_kernel, rows_n, cols_n), out_shap...]
    pallas_call x1, Pallas kernels: 22.5 us -> 21.2 us  [shards(): pl.pallas_call(functools.partial(update_kernel, wide, deep), grid=(wide +...]
where the time goes in v2:
time: 76.6 us; the launch traced here: 75.8 us
  Pallas kernels  75 us (98%)
  between operations  0.8 us (1%)
    pallas_call x1, Pallas kernels, shards(): pl.pallas_call(functools.partial(factor_kernel, rows_n, cols_n), out_shap...  53.7 us
    pallas_call x1, Pallas kernels, shards(): pl.pallas_call(functools.partial(update_kernel, wide, deep), grid=(wide +...  21.2 us

profile of v2, /device:TPU:24, one launch (start us, length us, event | category | flops | bytes accessed | tf_op | source)
XLA Modules:
  0.0 75.8 jit_solution(7010068147545421036)
XLA Ops:
  0.6 53.7 %factor.1 = (f32[512,512]{1,0:T(8,128)}, f32[512,512]{1,0:T(8,128)}, f32[512,512]{1,0:T(8,128)}, f32[1024,512]{1,0:T(8,128)}) custom-call(f32[64,512]{1,0:T(8,128)} %a_ref.1, f32[128,512]{1,0:T(8,128)} %pb_ref.1), custom_call_target="tpu_custom_call" | custom-call | tf_op jit(solution)/shard_map/factor/pallas_call | solution.py:386
  54.4 21.2 %update.1 = (f32[512,512]{1,0:T(8,128)}, f32[128,512]{1,0:T(8,128)}, f32[512,3072]{1,0:T(8,128)}, f32[512,3072]{1,0:T(8,128)}, f32[512,1024]{1,0:T(8,128)}) custom-call(f32[512,512]{1,0:T(8,128)} %get-tuple-element.14.l_ref, f32[512,512]{1,0:T(8,128)} %get-tuple-element.15.pr_ref, f32[1024,512]{1,0:T(8,128)} %get-tuple-element.16.pc_ref, ...), custom_call_target="tpu_custom_call" | custom-call | tf_op jit(solution)/shard_map/update/pallas_call | solution.py:405
